TPU v7x, 1024 devices: a whole 4x4x32 slice. The times are simulated.
1024 devices in a mesh: outer: 4 (over x), inner: 256 (over y, z, core).
Axes of the slice: x: 4, y: 4, z: 32, core: 2. Of those that a mesh axis runs over, the one named last changes fastest.
Arguments:
- image_emb: float32 [8192, 1152], P(('outer', 'inner')), may hold values from -0.27 to 0.27
- text_emb: float32 [8192, 1152], P(('outer', 'inner')), may hold values from -0.27 to 0.27
- labels: int32 [8192], replicated, may hold values from 0 to 8191, each once
- scale_logarithm: float32 [1], replicated, may hold values from 1 to 2
- bias: float32 [1], replicated, may hold values from -2 to -0.5
Outputs:
- image_grad: float32 [8192, 1152], P(('outer', 'inner'))
- text_grad: float32 [8192, 1152], P(('outer', 'inner'))
Inputs may be any that keep to these rules, and one draw needn't show every extreme that they name: `labels`: every text index is named by exactly one image.
All inputs are finite; a program needn't handle non-finite values.
Results may differ from a plain program's by a relative error of at most 0.0028.
Values may be sent and summed in bfloat16 or wider, within the bound.
A program may use at most 64 MiB of HBM per device.

v0:
```python
import jax
import jax.numpy as jnp
from jax import lax
from jax.sharding import PartitionSpec as P

epsilon = 1e-06


def normalize(values):
    length = jnp.sqrt(jnp.sum(values * values, axis=1, keepdims=True) + epsilon)
    return (values / length, length)


def unit_back(unit_rows, length, unit_grad):
    return (unit_grad - unit_rows * jnp.sum(unit_rows * unit_grad, axis=1, keepdims=True)) / length


def per_device(image_emb, text_emb, labels, scale_logarithm, bias):
    own_rows, feature_count = image_emb.shape
    outer_count = lax.axis_size("outer")
    inner_count = lax.axis_size("inner")
    group_texts = own_rows * inner_count
    outer_pos = lax.axis_index("outer")
    inner_pos = lax.axis_index("inner")
    group_first = outer_pos * group_texts
    logit_scale_factor = jnp.exp(scale_logarithm[0])
    logit_bias_value = bias[0]
    image_unit, image_len = normalize(image_emb)
    text_unit, text_len = normalize(text_emb)
    image_low = image_unit.astype(jnp.bfloat16)
    text_reduced_precision = text_unit.astype(jnp.bfloat16)
    images = lax.all_gather(image_low, "outer", axis=0, tiled=True)
    label_table = labels.reshape(outer_count, inner_count, own_rows)
    label_rows = lax.dynamic_slice_in_dim(label_table, inner_pos, 1, 1).reshape(
        outer_count * own_rows
    )
    text_portion = lax.all_gather(text_reduced_precision, "inner", axis=0, tiled=True)
    piece_rows = text_portion.shape[0]
    pair_similarity = jnp.einsum(
        "rd,cd->rc", images, text_portion, preferred_element_type=jnp.float32
    )
    pair_logit_matrix = logit_scale_factor * pair_similarity + logit_bias_value
    columns = group_first + jnp.arange(piece_rows, dtype=jnp.int32)
    target = jnp.where(label_rows[:, None] == columns[None, :], jnp.float32(1.0), jnp.float32(-1.0))
    weights = -target * jax.nn.sigmoid(-target * pair_logit_matrix)
    weight_reduced_precision = weights.astype(jnp.bfloat16)
    gradient_running = logit_scale_factor * jnp.dot(
        weight_reduced_precision, text_portion, preferred_element_type=jnp.float32
    )
    text_unit_grad = lax.psum_scatter(
        logit_scale_factor
        * jnp.einsum(
            "rc,rd->cd", weight_reduced_precision, images, preferred_element_type=jnp.float32
        ),
        "inner",
        scatter_dimension=0,
        tiled=True,
    )
    image_unit_grad = lax.psum_scatter(gradient_running, "outer", scatter_dimension=0, tiled=True)
    image_grad = unit_back(image_unit, image_len, image_unit_grad)
    text_grad = unit_back(text_unit, text_len, text_unit_grad)
    return (image_grad, text_grad)


def solution(mesh):
    placed = (P(("outer", "inner"), None), P(("outer", "inner"), None), P(), P(), P())
    return jax.shard_map(
        per_device,
        mesh=mesh,
        in_specs=placed,
        out_specs=(P(("outer", "inner"), None), P(("outer", "inner"), None)),
        check_vma=False,
    )
```

profile of v0, /device:TPU:6, one launch (start us, length us, event | category | flops | bytes accessed | tf_op | source)
XLA Modules:
  0.0 1074.7 jit_solution(1659529573358203151)
XLA Ops:
  7.2 0.0 all-gather.2.cloned.1.call-start
  7.2 0.9 multiply_reduce_fusion.2
  8.1 1.5 fusion.9
  9.6 0.0 all-gather.2.cloned.1.call-update
  9.6 0.0 all-reduce.5.cloned.1.call-start
  11.0 1.1 reshape.27
  12.1 0.1 eq.15
  12.2 0.9 multiply_reduce_fusion.3
  13.1 0.8 fusion.8
  13.9 21.8 %all_gather.6 = bf16[32,1152]{1,0:T(8,128)(2,1)S(1)} all-gather(bf16[8,1152]{1,0:T(8,128)(2,1)S(1)} %fusion.8), channel_id=1, replica_groups=mesh['outer'=4,'inner'=256] {'outer'}, dimensions={0}, use_global_device_ids=true | all-gather | bytes 92160 | tf_op jit(solution)/shard_map/all_gather | solution.py:32
  35.7 253.5 %all-gather.2.cloned.1.call-done = bf16[2048,1152]{1,0:T(8,128)(2,1)} async-done(((bf16[8,1152]{1,0:T(8,128)(2,1)}), bf16[2048,1152]{1,0:T(8,128)(2,1)}) %all-gather.2.cloned.1.call-update) | async-done | bytes 4718608 | tf_op jit(solution)/shard_map/all_gather | solution.py:37
  289.2 3.9 fusion.7
  293.0 3.9 convolution_multiply_fusion.1
  296.9 0.0 all-reduce.5.cloned.1.call-update
  297.0 0.0 copy-start
  297.0 0.0 copy-start.1
  297.0 0.0 all-reduce.7.cloned.1.call-start
  297.0 5.1 convolution_multiply_fusion
  302.1 0.0 all-reduce.7.cloned.1.call-update
  302.1 1.3 dynamic-slice.2
  303.4 1.3 dynamic-slice
  306.0 58.8 %all-reduce.5.cloned.1.call-done = f32[32,1152]{1,0:T(8,128)} async-done(((f32[32,1152]{1,0:T(8,128)}), f32[32,1152]{1,0:T(8,128)}) %all-reduce.5.cloned.1.call-update) | async-done | bytes 147472
  364.8 0.0 copy-done
  364.8 1.0 multiply_reduce_fusion.1
  365.7 1.5 subtract_divide_fusion.1
  367.2 698.6 %all-reduce.7.cloned.1.call-done = f32[2048,1152]{1,0:T(8,128)} async-done(((f32[2048,1152]{1,0:T(8,128)}), f32[2048,1152]{1,0:T(8,128)}) %all-reduce.7.cloned.1.call-update) | async-done | bytes 9437200
  1065.8 0.0 copy-done.1
  1065.8 1.0 multiply_reduce_fusion
  1066.7 1.5 subtract_divide_fusion
  (4 shorter events, 0.1 us)
Async XLA Ops:
  7.2 282.0 %all-gather.2.cloned.1.call-start = ((), (), s32[]{:S(2)}) async-start(), calls=%async_computation | async-start | bytes 4737024 | tf_op jit(solution)/shard_map/all_gather | solution.py:37
  9.6 355.2 %all-reduce.5.cloned.1.call-start = ((), (), s32[]{:S(2)}) async-start(), calls=%async_computation.1 | async-start | bytes 294912
  297.0 67.8 %copy-start = (f32[8,1152]{1,0:T(8,128)S(1)}, f32[8,1152]{1,0:T(8,128)}, u32[]{:S(2)}) copy-start(f32[8,1152]{1,0:T(8,128)} %param.5) | copy-start | bytes 110596
  297.0 768.8 %copy-start.1 = (f32[8,1152]{1,0:T(8,128)S(1)}, f32[8,1152]{1,0:T(8,128)}, u32[]{:S(2)}) copy-start(f32[8,1152]{1,0:T(8,128)} %param.6) | copy-start | bytes 110596
  297.0 768.8 %all-reduce.7.cloned.1.call-start = ((), (), s32[]{:S(2)}) async-start(), calls=%async_computation.2 | async-start | bytes 18874368
Sparse Core Ops, SparseCore 0:
  12.8 276.3 all-gather.1
  297.1 67.6 all-reduce.4
  368.6 697.1 all-reduce.6
where the time goes:
time: 1080 us; the launch traced here: 1070 us
  waiting for transfers between devices  1010 us (94%)
  blocking collectives  21.8 us (2%)
  between operations  16.4 us (2%)
  matrix products  12.8 us (1%)
    unnamed x5, waiting for transfers between devices  757 us
    all_gather x1, waiting for transfers between devices, per_device(): lax.all_gather(text_reduced_precision, 'inner', axis=0, tiled=True)  253 us
    all_gather x1, blocking collectives, per_device(): images = lax.all_gather(image_low, 'outer', axis=0, tiled=True)  21.8 us
  transfers between devices with their start and end apart: 3, of which 3 were waited for; matrix products, arithmetic and copies ran while one was open for 1% of the time, Pallas kernels for 0%

commit v1 on v0

v1 whole, which is shorter than its diff:
```python
import functools

import jax
import jax.numpy as jnp
from jax import lax
from jax.experimental import pallas as pl
from jax.experimental.pallas import tpu as pltpu
from jax.sharding import PartitionSpec as P

EPSILON = 1e-06
X, Y, Z = 4, 4, 32
TEXT_STEPS = (0, 1, -1, 2, -2, 3, -3, 4)
IMAGE_STEPS = (4, -4, 12, -12)
STAGE = 5
BF = jnp.bfloat16
F32 = jnp.float32


def kernel(
    labels_ref, scale_ref, bias_ref, image_ref, text_ref,
    image_out, text_out,
    own_image, tbuf, ibuf, tsend, isend, town, iown, tback, iback,
    tsum, isum, tlast, ilast,
    zt_s, zt_r, zi_s, zi_r, pt_s, pt_r, pi_s, pi_r,
    rt_s, rt_r, ri_s, ri_r, lt_s, lt_r, li_s, li_r,
):
    nk, no = len(TEXT_STEPS), len(IMAGE_STEPS)
    nq = 2 * Y
    rows, width = image_ref.shape
    x = lax.axis_index("outer")
    inner = lax.axis_index("inner")
    core = lax.rem(inner, 2)
    z = lax.rem(inner // 2, Z)
    y = inner // (2 * Z)
    side = 1 - 2 * core

    def device(dx=0, dy=0, dz=0, dc=0):
        place_y = lax.rem(y + dy + Y, Y)
        place_z = lax.rem(z + dz + Z, Z)
        place_c = lax.rem(core + dc, 2)
        return (lax.rem(x + dx + X, X), (place_y * Z + place_z) * 2 + place_c)

    def send(src, dst, send_sem, recv_sem, place):
        pltpu.make_async_remote_copy(
            src_ref=src, dst_ref=dst, send_sem=send_sem, recv_sem=recv_sem,
            device_id=place, device_id_type=pl.DeviceIdType.MESH,
        ).start()

    def wait(ref, sem):
        pltpu.make_async_copy(ref, ref, sem).wait()

    barrier = pltpu.get_barrier_semaphore()
    near = {abs(s) for s in TEXT_STEPS + IMAGE_STEPS if s}
    partners = [device(dz=d) for a in sorted(near, reverse=True) for d in {a % Z, -a % Z}]
    partners += [device(dx=j) for j in range(1, X)]
    partners += [device(dy=q // 2, dc=q % 2) for q in range(1, nq)]
    for place in partners:
        pl.semaphore_signal(barrier, inc=1, device_id=place, device_id_type=pl.DeviceIdType.MESH)

    def normalize(values):
        length = jnp.sqrt(jnp.sum(values * values, axis=1, keepdims=True) + EPSILON)
        return values / length, length

    image_unit, image_len = normalize(image_ref[...])
    text_unit, text_len = normalize(text_ref[...])
    own_image[...] = image_unit.astype(BF)
    tbuf[0, 0] = text_unit.astype(BF)
    scale = jnp.exp(jnp.full((1, 1), scale_ref[0], F32))

    pl.semaphore_wait(barrier, len(partners))

    if STAGE >= 1:
        work = [("i", o, s) for o, s in enumerate(IMAGE_STEPS)]
        work += [("t", k, s) for k, s in enumerate(TEXT_STEPS) if s]
        for what, slot, step in sorted(work, key=lambda w: -abs(w[2])):
            if what == "i":
                send(own_image, ibuf.at[0, slot], zi_s, zi_r.at[slot], device(dz=step))
            else:
                send(tbuf.at[0, 0], tbuf.at[0, slot], zt_s, zt_r.at[slot], device(dz=side * step))

    def spread_text(k):
        if k:
            wait(tbuf.at[0, k], zt_r.at[k])
        if STAGE >= 2:
            for j in range(1, X):
                send(tbuf.at[0, k], tbuf.at[j, k], pt_s, pt_r, device(dx=j))

    def spread_image(o):
        wait(ibuf.at[0, o], zi_r.at[o])
        if STAGE >= 2:
            for q in range(1, nq):
                send(ibuf.at[0, o], ibuf.at[q, o], pi_s, pi_r, device(dy=q // 2, dc=q % 2))

    if STAGE >= 1:
        work = [(abs(s), 0, k) for k, s in enumerate(TEXT_STEPS)]
        work += [(abs(s), 1, o) for o, s in enumerate(IMAGE_STEPS)]
        for _, what, slot in sorted(work):
            (spread_image if what else spread_text)(slot)

    if STAGE >= 2:
        wait(tbuf.at[1:], pt_r)
        wait(ibuf.at[1:], pi_r)

    if STAGE >= 3:
        texts = tbuf[...].astype(F32).reshape(X * nk * rows, width).astype(BF)
        images = ibuf[...].astype(F32).reshape(nq * no * rows, width).astype(BF)
        similarity = lax.dot_general(
            images, texts, (((1,), (1,)), ((), ())), preferred_element_type=F32
        )
        logits = scale * similarity + bias_ref[0]

        lane = lax.broadcasted_iota(jnp.int32, (rows, 128), 1)
        row = lax.broadcasted_iota(jnp.int32, (rows, 128), 0)
        pieces = []
        for q in range(nq):
            from_y = lax.rem(y - q // 2 + Y, Y)
            from_c = lax.rem(core + q % 2, 2)
            for step in IMAGE_STEPS:
                from_z = lax.rem(z - step + Z, Z)
                first = ((x * Y + from_y) * Z + from_z) * (2 * rows) + from_c * rows
                line = labels_ref[pl.ds(first // 128, 1), :]
                pick = lane == row + lax.rem(first, 128)
                pieces.append(jnp.where(pick, jnp.broadcast_to(line, (rows, 128)), 0))
        label = jnp.sum(jnp.concatenate(pieces, axis=0).astype(F32), axis=1, keepdims=True)

        spot = lax.broadcasted_iota(jnp.int32, (1, X * nk * rows), 1)
        at_row, at_k, at_j = spot % rows, (spot // rows) % nk, spot // (rows * nk)
        step_of = jnp.zeros_like(spot)
        for k, step in enumerate(TEXT_STEPS):
            step_of = jnp.where(at_k == k, step, step_of)
        from_x = lax.rem(x - at_j + X, X)
        from_z = lax.rem(z - side * step_of + Z, Z)
        column = (((from_x * Y + y) * Z + from_z) * 2 + core) * rows + at_row
        match = label == column.astype(F32)

        signed = jnp.where(match, -logits, logits)
        sigmoid = 1.0 / (1.0 + jnp.exp(-signed))
        weights = jnp.where(match, -sigmoid, sigmoid).astype(BF)

        grad = jnp.dot(weights, texts, preferred_element_type=F32)
        grad = grad.reshape(nq, no, rows, width)
        iown[...] = grad[0]
        isend[...] = grad[1:].astype(BF)
    if STAGE >= 4:
        for o in reversed(range(no)):
            for q in range(1, nq):
                send(isend.at[q - 1, o], iback.at[o, q - 1], ri_s, ri_r.at[o],
                     device(dy=-(q // 2), dc=q % 2))
    if STAGE >= 3:
        grad = lax.dot_general(
            weights, images, (((0,), (0,)), ((), ())), preferred_element_type=F32
        )
        grad = grad.reshape(X, nk, rows, width)
        town[...] = grad[0]
        tsend[...] = grad[1:].astype(BF)
    if STAGE >= 4:
        for k in reversed(range(nk)):
            for j in range(1, X):
                send(tsend.at[j - 1, k], tback.at[k, j - 1], rt_s, rt_r.at[k], device(dx=-j))

        def join_image(o):
            wait(iback.at[o], ri_r.at[o])
            total = iown[o] + jnp.sum(iback[o].astype(F32), axis=0)
            isum[o] = total.astype(BF)
            if STAGE >= 5:
                send(isum.at[o], ilast.at[o], li_s, li_r.at[o], device(dz=-IMAGE_STEPS[o]))

        def join_text(k):
            wait(tback.at[k], rt_r.at[k])
            total = town[k] + jnp.sum(tback[k].astype(F32), axis=0)
            if k == 0:
                town[0] = total
            else:
                tsum[k - 1] = total.astype(BF)
                if STAGE >= 5:
                    send(tsum.at[k - 1], tlast.at[k - 1], lt_s, lt_r.at[k - 1],
                         device(dz=-side * TEXT_STEPS[k]))

        for o in reversed(range(no)):
            join_image(o)
        for k in reversed(range(nk)):
            join_text(k)

    def unit_back(unit, length, unit_grad):
        return (unit_grad - unit * jnp.sum(unit * unit_grad, axis=1, keepdims=True)) / length

    if STAGE >= 5:
        for o in range(no):
            wait(ilast.at[o], li_r.at[o])
        image_unit_grad = scale * jnp.sum(ilast[...].astype(F32), axis=0)
        image_out[...] = unit_back(image_unit, image_len, image_unit_grad)
        for k in range(nk - 1):
            wait(tlast.at[k], lt_r.at[k])
        text_unit_grad = scale * (town[0] + jnp.sum(tlast[...].astype(F32), axis=0))
        text_out[...] = unit_back(text_unit, text_len, text_unit_grad)
    else:
        image_out[...] = image_unit
        text_out[...] = text_unit

    if STAGE >= 1:
        wait(ibuf.at[0], zi_s)
        wait(tbuf.at[0, 1:], zt_s)
    if STAGE >= 2:
        wait(tbuf.at[1:], pt_s)
        wait(ibuf.at[1:], pi_s)
    if STAGE >= 4:
        wait(isend, ri_s)
        wait(tsend, rt_s)
    if STAGE >= 5:
        wait(isum, li_s)
        wait(tsum, lt_s)


def per_device(image_emb, text_emb, labels, scale_logarithm, bias):
    rows, width = image_emb.shape
    nk, no, nq = len(TEXT_STEPS), len(IMAGE_STEPS), 2 * Y
    block = (rows, width)
    vmem = pl.BlockSpec(memory_space=pltpu.VMEM)
    smem = pl.BlockSpec(memory_space=pltpu.SMEM)
    one = pltpu.SemaphoreType.DMA
    some = lambda n: pltpu.SemaphoreType.DMA((n,))
    return pl.pallas_call(
        kernel,
        out_shape=[jax.ShapeDtypeStruct(block, F32)] * 2,
        in_specs=[vmem, smem, smem, vmem, vmem],
        out_specs=[vmem, vmem],
        scratch_shapes=[
            pltpu.VMEM(block, BF),
            pltpu.VMEM((X, nk) + block, BF),
            pltpu.VMEM((nq, no) + block, BF),
            pltpu.VMEM((X - 1, nk) + block, BF),
            pltpu.VMEM((nq - 1, no) + block, BF),
            pltpu.VMEM((nk,) + block, F32),
            pltpu.VMEM((no,) + block, F32),
            pltpu.VMEM((nk, X - 1) + block, BF),
            pltpu.VMEM((no, nq - 1) + block, BF),
            pltpu.VMEM((nk - 1,) + block, BF),
            pltpu.VMEM((no,) + block, BF),
            pltpu.VMEM((nk - 1,) + block, BF),
            pltpu.VMEM((no,) + block, BF),
            one, some(nk), one, some(no),
            one, one, one, one,
            one, some(nk), one, some(no),
            one, some(nk - 1), one, some(no),
        ],
        compiler_params=pltpu.CompilerParams(
            collective_id=0, has_side_effects=True, vmem_limit_bytes=48 * 2**20
        ),
    )(labels.reshape(-1, 128), scale_logarithm, bias, image_emb, text_emb)


def solution(mesh):
    rows = P(("outer", "inner"), None)
    return jax.shard_map(
        per_device,
        mesh=mesh,
        in_specs=(rows, rows, P(), P(), P()),
        out_specs=(rows, rows),
        check_vma=False,
    )
```

time: 1080 us -> 72.4 us (0.07)
  the two profiles are of different devices: /device:TPU:6 before, /device:TPU:32 now
where the time goes in v1:
time: 72.4 us; the launch traced here: 72 us
  Pallas kernels  66.5 us (92%)
  local copies, waits for them, and re-layouts  3.52 us (5%)
  between operations  1.94 us (3%)
    pallas_call x1, Pallas kernels, per_device(): pl.pallas_call(kernel, out_shape=[jax.ShapeDtypeStruct(block, F32)] * 2,...  66.5 us
    unnamed x8, local copies, waits for them, and re-layouts  3.52 us

profile of v1, /device:TPU:32, one launch (start us, length us, event | category | flops | bytes accessed | tf_op | source)
XLA Modules:
  0.0 72.0 jit_solution(6513841328628086951)
XLA Ops:
  1.9 0.0 copy-start
  1.9 0.8 %copy-done = f32[8,1152]{1,0:T(8,128)S(1)} copy-done((f32[8,1152]{1,0:T(8,128)S(1)}, f32[8,1152]{1,0:T(8,128)}, u32[]{:S(2)}) %copy-start) | copy-done | bytes 36888
  2.7 0.0 copy-start.1
  2.7 0.8 %copy-done.1 = f32[8,1152]{1,0:T(8,128)S(1)} copy-done((f32[8,1152]{1,0:T(8,128)S(1)}, f32[8,1152]{1,0:T(8,128)}, u32[]{:S(2)}) %copy-start.1) | copy-done | bytes 36888
  3.5 0.0 copy-start.2
  3.5 0.8 %copy-done.2 = s32[8192]{0:T(1024)S(1)} copy-done((s32[8192]{0:T(1024)S(1)}, s32[8192]{0:T(1024)}, u32[]{:S(2)}) %copy-start.2) | copy-done | bytes 32792
  4.2 66.5 %shard_map.68 = (f32[8,1152]{1,0:T(8,128)S(1)}, f32[8,1152]{1,0:T(8,128)S(1)}) custom-call(s32[64,128]{1,0:T(8,128)S(1)} %bitcast.1, f32[1]{0:T(128)S(6)} %copy.9.scale_ref, f32[1]{0:T(128)S(6)} %copy.10.bias_ref, f32[8,1152]{1,0:T(8,128)S(1)} %copy-done, f32[8,1152]{1,0:T(8,128)S(1)} %copy-done.1), custom_call_target="tpu_custom_call" | custom-call | tf_op jit(solution)/shard_map/pallas_call | solution.py:222
  70.8 0.6 copy.11
  71.4 0.6 copy.12
Async XLA Ops:
  1.9 0.8 %copy-start = (f32[8,1152]{1,0:T(8,128)S(1)}, f32[8,1152]{1,0:T(8,128)}, u32[]{:S(2)}) copy-start(f32[8,1152]{1,0:T(8,128)} %image_ref.1) | copy-start | bytes 110596
  2.7 0.8 %copy-start.1 = (f32[8,1152]{1,0:T(8,128)S(1)}, f32[8,1152]{1,0:T(8,128)}, u32[]{:S(2)}) copy-start(f32[8,1152]{1,0:T(8,128)} %text_ref.1) | copy-start | bytes 110596
  3.5 0.8 %copy-start.2 = (s32[8192]{0:T(1024)S(1)}, s32[8192]{0:T(1024)}, u32[]{:S(2)}) copy-start(s32[8192]{0:T(1024)} %param.7) | copy-start | bytes 98308

commit v2 on v1

--- a/solution.py
+++ b/solution.py
@@ -9,24 +9,36 @@
 
 EPSILON = 1e-06
 X, Y, Z = 4, 4, 32
-TEXT_STEPS = (0, 1, -1, 2, -2, 3, -3, 4)
-IMAGE_STEPS = (4, -4, 12, -12)
+STRIDE = 4
+TEXT_STEPS = (4, 3, 2, 1, 0, -1, -2, -3)
+IMAGE_STEPS = (12, 4, -4, -12)
 STAGE = 5
 BF = jnp.bfloat16
 F32 = jnp.float32
 
 
 def kernel(
-    labels_ref, scale_ref, bias_ref, image_ref, text_ref,
+    labels_hbm, scale_hbm, bias_hbm, image_hbm, text_hbm,
     image_out, text_out,
     own_image, tbuf, ibuf, tsend, isend, town, iown, tback, iback,
     tsum, isum, tlast, ilast,
     zt_s, zt_r, zi_s, zi_r, pt_s, pt_r, pi_s, pi_r,
     rt_s, rt_r, ri_s, ri_r, lt_s, lt_r, li_s, li_r,
+    image_ref, text_ref, labels_ref, scale_ref, bias_ref, load, relay, relay_r,
 ):
     nk, no = len(TEXT_STEPS), len(IMAGE_STEPS)
     nq = 2 * Y
+    home = TEXT_STEPS.index(0)
     rows, width = image_ref.shape
+    loads = [
+        pltpu.make_async_copy(src, dst, load.at[n])
+        for n, (src, dst) in enumerate(
+            ((image_hbm, image_ref), (text_hbm, text_ref), (labels_hbm, labels_ref),
+             (scale_hbm, scale_ref), (bias_hbm, bias_ref))
+        )
+    ]
+    for copy in loads:
+        copy.start()
     x = lax.axis_index("outer")
     inner = lax.axis_index("inner")
     core = lax.rem(inner, 2)
@@ -50,7 +62,7 @@
         pltpu.make_async_copy(ref, ref, sem).wait()
 
     barrier = pltpu.get_barrier_semaphore()
-    near = {abs(s) for s in TEXT_STEPS + IMAGE_STEPS if s}
+    near = {abs(s) for s in TEXT_STEPS if s}
     partners = [device(dz=d) for a in sorted(near, reverse=True) for d in {a % Z, -a % Z}]
     partners += [device(dx=j) for j in range(1, X)]
     partners += [device(dy=q // 2, dc=q % 2) for q in range(1, nq)]
@@ -61,41 +73,56 @@
         length = jnp.sqrt(jnp.sum(values * values, axis=1, keepdims=True) + EPSILON)
         return values / length, length
 
+    for copy in loads:
+        copy.wait()
     image_unit, image_len = normalize(image_ref[...])
     text_unit, text_len = normalize(text_ref[...])
     own_image[...] = image_unit.astype(BF)
-    tbuf[0, 0] = text_unit.astype(BF)
+    tbuf[0, home] = text_unit.astype(BF)
     scale = jnp.exp(jnp.full((1, 1), scale_ref[0], F32))
 
     pl.semaphore_wait(barrier, len(partners))
 
-    if STAGE >= 1:
-        work = [("i", o, s) for o, s in enumerate(IMAGE_STEPS)]
-        work += [("t", k, s) for k, s in enumerate(TEXT_STEPS) if s]
-        for what, slot, step in sorted(work, key=lambda w: -abs(w[2])):
-            if what == "i":
-                send(own_image, ibuf.at[0, slot], zi_s, zi_r.at[slot], device(dz=step))
-            else:
-                send(tbuf.at[0, 0], tbuf.at[0, slot], zt_s, zt_r.at[slot], device(dz=side * step))
-
     def spread_text(k):
-        if k:
-            wait(tbuf.at[0, k], zt_r.at[k])
         if STAGE >= 2:
             for j in range(1, X):
                 send(tbuf.at[0, k], tbuf.at[j, k], pt_s, pt_r, device(dx=j))
 
     def spread_image(o):
-        wait(ibuf.at[0, o], zi_r.at[o])
         if STAGE >= 2:
             for q in range(1, nq):
                 send(ibuf.at[0, o], ibuf.at[q, o], pi_s, pi_r, device(dy=q // 2, dc=q % 2))
 
     if STAGE >= 1:
-        work = [(abs(s), 0, k) for k, s in enumerate(TEXT_STEPS)]
-        work += [(abs(s), 1, o) for o, s in enumerate(IMAGE_STEPS)]
-        for _, what, slot in sorted(work):
-            (spread_image if what else spread_text)(slot)
+        for o, step in ((1, STRIDE), (2, -STRIDE)):
+            send(own_image, ibuf.at[0, o], zi_s, zi_r.at[o], device(dz=step))
+        for k, step in sorted(enumerate(TEXT_STEPS), key=lambda w: abs(w[1])):
+            if step:
+                send(tbuf.at[0, home], tbuf.at[0, k], zt_s, zt_r.at[k], device(dz=side * step))
+        spread_text(home)
+
+        def pull_text(k):
+            wait(tbuf.at[0, k], zt_r.at[k])
+            spread_text(k)
+
+        for k, step in enumerate(TEXT_STEPS):
+            if 0 < abs(step) <= STRIDE // 2:
+                pull_text(k)
+        for o, step in ((1, STRIDE), (2, -STRIDE)):
+            wait(ibuf.at[0, o], zi_r.at[o])
+            send(ibuf.at[0, o], relay.at[o - 1], zi_s, relay_r.at[o - 1], device(dz=step))
+        for o in (1, 2):
+            spread_image(o)
+        for k, step in enumerate(TEXT_STEPS):
+            if STRIDE // 2 < abs(step):
+                pull_text(k)
+        for o, step in ((1, STRIDE), (2, -STRIDE)):
+            wait(relay.at[o - 1], relay_r.at[o - 1])
+            far = 0 if o == 1 else 3
+            send(relay.at[o - 1], ibuf.at[0, far], zi_s, zi_r.at[far], device(dz=step))
+        for o in (0, 3):
+            wait(ibuf.at[0, o], zi_r.at[o])
+            spread_image(o)
 
     if STAGE >= 2:
         wait(tbuf.at[1:], pt_r)
@@ -141,8 +168,16 @@
         grad = grad.reshape(nq, no, rows, width)
         iown[...] = grad[0]
         isend[...] = grad[1:].astype(BF)
+    low = lax.rem(z - IMAGE_STEPS[0] + Z, Z)
+    first_image = (Z + 2 * STRIDE - 1 - low) // (2 * STRIDE)
+    image_turns = [lax.rem(first_image + n, no) for n in range(no)]
+    low = lax.rem(z - STRIDE + core + Z, Z)
+    first_text = jnp.where(low > Z - nk, Z - low, 0)
+    turn = [lax.rem(first_text + n, nk) for n in range(nk)]
+    text_turns = [jnp.where(core == 0, n, nk - 1 - n) for n in turn]
+
     if STAGE >= 4:
-        for o in reversed(range(no)):
+        for o in image_turns:
             for q in range(1, nq):
                 send(isend.at[q - 1, o], iback.at[o, q - 1], ri_s, ri_r.at[o],
                      device(dy=-(q // 2), dc=q % 2))
@@ -154,7 +189,7 @@
         town[...] = grad[0]
         tsend[...] = grad[1:].astype(BF)
     if STAGE >= 4:
-        for k in reversed(range(nk)):
+        for k in text_turns:
             for j in range(1, X):
                 send(tsend.at[j - 1, k], tback.at[k, j - 1], rt_s, rt_r.at[k], device(dx=-j))
 
@@ -163,23 +198,30 @@
             total = iown[o] + jnp.sum(iback[o].astype(F32), axis=0)
             isum[o] = total.astype(BF)
             if STAGE >= 5:
-                send(isum.at[o], ilast.at[o], li_s, li_r.at[o], device(dz=-IMAGE_STEPS[o]))
+                send(isum.at[o], ilast.at[o], li_s, li_r.at[o],
+                     device(dz=2 * STRIDE * o - IMAGE_STEPS[0]))
 
         def join_text(k):
             wait(tback.at[k], rt_r.at[k])
             total = town[k] + jnp.sum(tback[k].astype(F32), axis=0)
-            if k == 0:
-                town[0] = total
-            else:
-                tsum[k - 1] = total.astype(BF)
+            tsum[k] = total.astype(BF)
+
+            @pl.when(k == home)
+            def _():
+                town[home] = total
+
+            @pl.when(k != home)
+            def _():
                 if STAGE >= 5:
-                    send(tsum.at[k - 1], tlast.at[k - 1], lt_s, lt_r.at[k - 1],
-                         device(dz=-side * TEXT_STEPS[k]))
-
-        for o in reversed(range(no)):
+                    send(tsum.at[k], tlast.at[k], lt_s, lt_r.at[k], device(dz=side * (k - STRIDE)))
+
+        join_image(image_turns[0])
+        for n in range(nk):
+            join_text(text_turns[n])
+            if n == nk // 2:
+                join_image(image_turns[1])
+        for o in image_turns[2:]:
             join_image(o)
-        for k in reversed(range(nk)):
-            join_text(k)
 
     def unit_back(unit, length, unit_grad):
         return (unit_grad - unit * jnp.sum(unit * unit_grad, axis=1, keepdims=True)) / length
@@ -189,9 +231,10 @@
             wait(ilast.at[o], li_r.at[o])
         image_unit_grad = scale * jnp.sum(ilast[...].astype(F32), axis=0)
         image_out[...] = unit_back(image_unit, image_len, image_unit_grad)
-        for k in range(nk - 1):
+        others = [k for k in range(nk) if k != home]
+        for k in others:
             wait(tlast.at[k], lt_r.at[k])
-        text_unit_grad = scale * (town[0] + jnp.sum(tlast[...].astype(F32), axis=0))
+        text_unit_grad = scale * sum((tlast[k].astype(F32) for k in others), town[home])
         text_out[...] = unit_back(text_unit, text_len, text_unit_grad)
     else:
         image_out[...] = image_unit
@@ -199,6 +242,7 @@
 
     if STAGE >= 1:
         wait(ibuf.at[0], zi_s)
+        wait(relay, zi_s)
         wait(tbuf.at[0, 1:], zt_s)
     if STAGE >= 2:
         wait(tbuf.at[1:], pt_s)
@@ -208,7 +252,7 @@
         wait(tsend, rt_s)
     if STAGE >= 5:
         wait(isum, li_s)
-        wait(tsum, lt_s)
+        wait(tsum.at[1:], lt_s)
 
 
 def per_device(image_emb, text_emb, labels, scale_logarithm, bias):
@@ -216,13 +260,13 @@
     nk, no, nq = len(TEXT_STEPS), len(IMAGE_STEPS), 2 * Y
     block = (rows, width)
     vmem = pl.BlockSpec(memory_space=pltpu.VMEM)
-    smem = pl.BlockSpec(memory_space=pltpu.SMEM)
+    hbm = pl.BlockSpec(memory_space=pltpu.HBM)
     one = pltpu.SemaphoreType.DMA
     some = lambda n: pltpu.SemaphoreType.DMA((n,))
     return pl.pallas_call(
         kernel,
         out_shape=[jax.ShapeDtypeStruct(block, F32)] * 2,
-        in_specs=[vmem, smem, smem, vmem, vmem],
+        in_specs=[hbm] * 5,
         out_specs=[vmem, vmem],
         scratch_shapes=[
             pltpu.VMEM(block, BF),
@@ -234,17 +278,25 @@
             pltpu.VMEM((no,) + block, F32),
             pltpu.VMEM((nk, X - 1) + block, BF),
             pltpu.VMEM((no, nq - 1) + block, BF),
-            pltpu.VMEM((nk - 1,) + block, BF),
+            pltpu.VMEM((nk,) + block, BF),
             pltpu.VMEM((no,) + block, BF),
-            pltpu.VMEM((nk - 1,) + block, BF),
+            pltpu.VMEM((nk,) + block, BF),
             pltpu.VMEM((no,) + block, BF),
             one, some(nk), one, some(no),
             one, one, one, one,
             one, some(nk), one, some(no),
-            one, some(nk - 1), one, some(no),
+            one, some(nk), one, some(no),
+            pltpu.VMEM(block, F32),
+            pltpu.VMEM(block, F32),
+            pltpu.VMEM((labels.shape[0] // 128, 128), jnp.int32),
+            pltpu.SMEM((1,), F32),
+            pltpu.SMEM((1,), F32),
+            some(5),
+            pltpu.VMEM((2,) + block, BF),
+            some(2),
         ],
         compiler_params=pltpu.CompilerParams(
-            collective_id=0, has_side_effects=True, vmem_limit_bytes=48 * 2**20
+            collective_id=0, has_side_effects=True, vmem_limit_bytes=60 * 2**20
         ),
     )(labels.reshape(-1, 128), scale_logarithm, bias, image_emb, text_emb)
 

time: 72.4 us -> 65.6 us (0.906)
  the two profiles are of different devices: /device:TPU:32 before, /device:TPU:2 now
where the time goes in v2:
time: 65.6 us; the launch traced here: 65.3 us
  Pallas kernels  61.3 us (93%)
  local copies, waits for them, and re-layouts  2.01 us (3%)
  between operations  1.94 us (3%)
    pallas_call x1, Pallas kernels, per_device(): pl.pallas_call(kernel, out_shape=[jax.ShapeDtypeStruct(block, F32)] * 2,...  61.3 us
    unnamed x4, local copies, waits for them, and re-layouts  2.01 us

profile of v2, /device:TPU:2, one launch (start us, length us, event | category | flops | bytes accessed | tf_op | source)
XLA Modules:
  0.0 65.3 jit_solution(16277673444630757839)
XLA Ops:
  1.9 61.3 %shard_map.68 = (f32[8,1152]{1,0:T(8,128)}, f32[8,1152]{1,0:T(8,128)}) custom-call(s32[64,128]{1,0:T(8,128)} %bitcast.1, f32[1]{0:T(128)S(6)} %copy.9.scale_hbm, f32[1]{0:T(128)S(6)} %copy.10.bias_hbm, f32[8,1152]{1,0:T(8,128)} %image_hbm.1, f32[8,1152]{1,0:T(8,128)} %text_hbm.1), custom_call_target="tpu_custom_call" | custom-call | tf_op jit(solution)/shard_map/pallas_call | solution.py:266
  63.3 0.0 copy-start
  63.3 1.4 %copy.11 = f32[8,1152]{1,0:T(8,128)} copy(f32[8,1152]{1,0:T(8,128)} %get-tuple-element.4) | data formatting | bytes 73728
  64.7 0.0 copy-done
  64.7 0.6 copy.12
Async XLA Ops:
  63.3 1.4 %copy-start = (f32[8,1152]{1,0:T(8,128)S(1)}, f32[8,1152]{1,0:T(8,128)}, u32[]{:S(2)}) copy-start(f32[8,1152]{1,0:T(8,128)} %get-tuple-element.5) | copy-start | bytes 110596

commit v3 on v2

v3 whole, which is shorter than its diff:
```python
import functools

import jax
import jax.numpy as jnp
from jax import lax
from jax.experimental import pallas as pl
from jax.experimental.pallas import tpu as pltpu
from jax.sharding import PartitionSpec as P

EPSILON = 1e-06
X, Y, Z = 4, 4, 32
STRIDE = 4
TEXT_STEPS = (4, 3, 2, 1, 0, -1, -2, -3)
IMAGE_STEPS = (12, 4, -4, -12)
BF = jnp.bfloat16
F32 = jnp.float32


def kernel(
    labels_hbm, scale_hbm, bias_hbm, image_hbm, text_hbm,
    image_out, text_out,
    own_image, tbuf, ibuf, tsend, isend, town, iown, tback, iback,
    tsum, isum, tlast, ilast,
    zt_s, zt_r, zi_s, zi_r, pt_s, pt_r, pi_s, pi_r,
    rt_s, rt_r, ri_s, ri_r, lt_s, lt_r, li_s, li_r,
    image_ref, text_ref, labels_ref, scale_ref, bias_ref, load, tnear, ready,
):
    nk, no = len(TEXT_STEPS), len(IMAGE_STEPS)
    nq = 2 * Y
    home = TEXT_STEPS.index(0)
    rows, width = image_ref.shape
    loads = [
        pltpu.make_async_copy(src, dst, load.at[n])
        for n, (src, dst) in enumerate(
            ((image_hbm, image_ref), (text_hbm, text_ref), (labels_hbm, labels_ref),
             (scale_hbm, scale_ref), (bias_hbm, bias_ref))
        )
    ]
    for copy in loads:
        copy.start()
    x = lax.axis_index("outer")
    inner = lax.axis_index("inner")
    core = lax.rem(inner, 2)
    z = lax.rem(inner // 2, Z)
    y = inner // (2 * Z)
    side = 1 - 2 * core

    def device(dx=0, dy=0, dz=0, dc=0):
        place_y = lax.rem(y + dy + Y, Y)
        place_z = lax.rem(z + dz + Z, Z)
        place_c = lax.rem(core + dc, 2)
        return (lax.rem(x + dx + X, X), (place_y * Z + place_z) * 2 + place_c)

    def send(src, dst, send_sem, recv_sem, place):
        pltpu.make_async_remote_copy(
            src_ref=src, dst_ref=dst, send_sem=send_sem, recv_sem=recv_sem,
            device_id=place, device_id_type=pl.DeviceIdType.MESH,
        ).start()

    def wait(ref, sem):
        pltpu.make_async_copy(ref, ref, sem).wait()

    barrier = pltpu.get_barrier_semaphore()
    near = {abs(s) for s in TEXT_STEPS if s}
    partners = [device(dz=d) for a in sorted(near, reverse=True) for d in {a % Z, -a % Z}]
    partners += [device(dx=j) for j in range(1, X)]
    partners += [device(dy=q // 2, dc=q % 2) for q in range(1, nq)]
    for place in partners:
        pl.semaphore_signal(barrier, inc=1, device_id=place, device_id_type=pl.DeviceIdType.MESH)

    def normalize(values):
        length = jnp.sqrt(jnp.sum(values * values, axis=1, keepdims=True) + EPSILON)
        return values / length, length

    for copy in loads:
        copy.wait()
    image_unit, image_len = normalize(image_ref[...])
    text_unit, text_len = normalize(text_ref[...])
    own_image[...] = image_unit.astype(BF)
    tbuf[0, home] = text_unit.astype(BF)
    scale = jnp.exp(jnp.full((1, 1), scale_ref[0], F32))

    pl.semaphore_wait(barrier, len(partners))

    def spread_text(k):
        for j in range(1, X):
            send(tbuf.at[0, k], tbuf.at[j, k], pt_s, pt_r, device(dx=j))

    def spread_image(o):
        for q in range(1, nq):
            send(ibuf.at[o, 0], ibuf.at[o, q], pi_s, pi_r.at[o], device(dy=q // 2, dc=q % 2))

    for o, step in ((1, STRIDE), (2, -STRIDE)):
        send(own_image, ibuf.at[o, 0], zi_s, zi_r.at[o], device(dz=step))
        pl.semaphore_signal(
            ready.at[2 - o], inc=1, device_id=device(dz=step),
            device_id_type=pl.DeviceIdType.MESH,
        )
    for k, step in sorted(enumerate(TEXT_STEPS), key=lambda w: abs(w[1])):
        if step:
            send(tbuf.at[0, home], tbuf.at[0, k], zt_s, zt_r.at[k], device(dz=side * step))
    spread_text(home)

    lane = lax.broadcasted_iota(jnp.int32, (rows, 128), 1)
    row = lax.broadcasted_iota(jnp.int32, (rows, 128), 0)

    def label_of(step):
        pieces = []
        for q in range(nq):
            from_y = lax.rem(y - q // 2 + Y, Y)
            from_c = lax.rem(core + q % 2, 2)
            from_z = lax.rem(z - step + Z, Z)
            first = ((x * Y + from_y) * Z + from_z) * (2 * rows) + from_c * rows
            line = labels_ref[pl.ds(first // 128, 1), :]
            pick = lane == row + lax.rem(first, 128)
            pieces.append(jnp.where(pick, jnp.broadcast_to(line, (rows, 128)), 0))
        pieces = jnp.concatenate(pieces, axis=0).astype(F32)
        return jnp.sum(pieces, axis=1, keepdims=True)

    swap = lax.rem(z + IMAGE_STEPS[0], Z) < lax.rem(z - IMAGE_STEPS[0] + Z, Z)
    far_turns = [jnp.where(swap, 3, 0), jnp.where(swap, 0, 3)]
    near_label = jnp.concatenate([label_of(STRIDE), label_of(-STRIDE)], axis=0)
    far_labels = [label_of(IMAGE_STEPS[0] - 2 * STRIDE * o) for o in far_turns]

    spot = lax.broadcasted_iota(jnp.int32, (1, X * nk * rows), 1)
    at_row, at_k, at_j = spot % rows, (spot // rows) % nk, spot // (rows * nk)
    from_x = lax.rem(x - at_j + X, X)
    from_z = lax.rem(z - side * (STRIDE - at_k) + Z, Z)
    column = (((from_x * Y + y) * Z + from_z) * 2 + core) * rows + at_row
    column = column.astype(F32)

    def as_rows(block):
        return block.astype(F32).reshape(-1, width).astype(BF)

    def weigh(images, texts, label):
        similarity = lax.dot_general(
            images, texts, (((1,), (1,)), ((), ())), preferred_element_type=F32
        )
        logits = scale * similarity + bias_ref[0]
        match = label == column
        signed = jnp.where(match, -logits, logits)
        sigmoid = 1.0 / (1.0 + jnp.exp(-signed))
        return jnp.where(match, -sigmoid, sigmoid).astype(BF)

    def keep_images(grad, slots):
        grad = grad.reshape(len(slots), nq, rows, width)
        for n, o in enumerate(slots):
            iown[o] = grad[n, 0]
            isend[o] = grad[n, 1:].astype(BF)

    def return_image(o):
        for q in range(1, nq):
            send(isend.at[o, q - 1], iback.at[o, q - 1], ri_s, ri_r.at[o],
                 device(dy=-(q // 2), dc=q % 2))

    def join_image(o):
        wait(iback.at[o], ri_r.at[o])
        total = iown[o] + jnp.sum(iback[o].astype(F32), axis=0)
        isum[o] = total.astype(BF)
        send(isum.at[o], ilast.at[o], li_s, li_r.at[o],
             device(dz=2 * STRIDE * o - IMAGE_STEPS[0]))

    def pull_text(k):
        wait(tbuf.at[0, k], zt_r.at[k])
        spread_text(k)

    for k, step in enumerate(TEXT_STEPS):
        if 0 < abs(step) <= STRIDE // 2:
            pull_text(k)
    for o, step in ((1, STRIDE), (2, -STRIDE)):
        wait(ibuf.at[o, 0], zi_r.at[o])
        pl.semaphore_wait(ready.at[o - 1], 1)
        far = 0 if o == 1 else 3
        send(ibuf.at[o, 0], ibuf.at[far, 0], zi_s, zi_r.at[far], device(dz=2 * step))
    for o in (1, 2):
        spread_image(o)
    for k, step in enumerate(TEXT_STEPS):
        if STRIDE // 2 < abs(step):
            pull_text(k)

    def pull_far():
        for o in far_turns:
            wait(ibuf.at[o, 0], zi_r.at[o])
            spread_image(o)

    pull_far()

    wait(tbuf.at[1:], pt_r)
    for o in (1, 2):
        wait(ibuf.at[o, 1:], pi_r.at[o])
    texts = as_rows(tbuf[...])
    images = as_rows(ibuf[1:3])
    weights = weigh(images, texts, near_label)
    keep_images(jnp.dot(weights, texts, preferred_element_type=F32), (1, 2))
    return_image(1)
    return_image(2)
    tnear[...] = lax.dot_general(
        weights, images, (((0,), (0,)), ((), ())), preferred_element_type=F32
    )
    urgent_low = jnp.logical_and(z >= STRIDE, z < 3 * STRIDE)
    urgent_high = jnp.logical_or(z < STRIDE, z >= Z - STRIDE)
    urgent_far = jnp.logical_and(z >= 3 * STRIDE, z < Z - STRIDE)

    for n, o in enumerate(far_turns):
        wait(ibuf.at[o, 1:], pi_r.at[o])
        images = as_rows(ibuf[o])
        weights = weigh(images, texts, far_labels[n])
        keep_images(jnp.dot(weights, texts, preferred_element_type=F32), (o,))
        return_image(o)
        tnear[...] += lax.dot_general(
            weights, images, (((0,), (0,)), ((), ())), preferred_element_type=F32
        )

    low = lax.rem(z - STRIDE + core + Z, Z)
    first_text = jnp.where(low > Z - nk, Z - low, 0)
    turn = [lax.rem(first_text + n, nk) for n in range(nk)]
    text_turns = [jnp.where(core == 0, n, nk - 1 - n) for n in turn]

    grad = tnear[...].reshape(X, nk, rows, width)
    town[...] = grad[0]
    tsend[...] = grad[1:].astype(BF)
    for k in text_turns:
        for j in range(1, X):
            send(tsend.at[j - 1, k], tback.at[k, j - 1], rt_s, rt_r.at[k], device(dx=-j))

    def join_text(k):
        wait(tback.at[k], rt_r.at[k])
        total = town[k] + jnp.sum(tback[k].astype(F32), axis=0)
        tsum[k] = total.astype(BF)

        @pl.when(k == home)
        def _():
            town[home] = total

        @pl.when(k != home)
        def _():
            send(tsum.at[k], tlast.at[k], lt_s, lt_r.at[k], device(dz=side * (k - STRIDE)))

    @pl.when(urgent_far)
    def _():
        join_image(far_turns[0])

    @pl.when(urgent_low)
    def _():
        join_image(1)

    @pl.when(urgent_high)
    def _():
        join_image(2)

    for n in range(nk):
        join_text(text_turns[n])

    @pl.when(jnp.logical_not(urgent_far))
    def _():
        join_image(far_turns[0])

    join_image(far_turns[1])

    @pl.when(jnp.logical_not(urgent_low))
    def _():
        join_image(1)

    @pl.when(jnp.logical_not(urgent_high))
    def _():
        join_image(2)

    def unit_back(unit, length, unit_grad):
        return (unit_grad - unit * jnp.sum(unit * unit_grad, axis=1, keepdims=True)) / length

    for o in range(no):
        wait(ilast.at[o], li_r.at[o])
    image_unit_grad = scale * jnp.sum(ilast[...].astype(F32), axis=0)
    image_out[...] = unit_back(image_unit, image_len, image_unit_grad)
    others = [k for k in range(nk) if k != home]
    for k in others:
        wait(tlast.at[k], lt_r.at[k])
    text_unit_grad = scale * sum((tlast[k].astype(F32) for k in others), town[home])
    text_out[...] = unit_back(text_unit, text_len, text_unit_grad)
    wait(isum, zi_s)
    wait(tbuf.at[0, 1:], zt_s)
    wait(tbuf.at[1:], pt_s)
    wait(iback, pi_s)
    wait(isend, ri_s)
    wait(tsend, rt_s)
    wait(isum, li_s)
    wait(tsum.at[1:], lt_s)


def per_device(image_emb, text_emb, labels, scale_logarithm, bias):
    rows, width = image_emb.shape
    nk, no, nq = len(TEXT_STEPS), len(IMAGE_STEPS), 2 * Y
    block = (rows, width)
    vmem = pl.BlockSpec(memory_space=pltpu.VMEM)
    hbm = pl.BlockSpec(memory_space=pltpu.HBM)
    one = pltpu.SemaphoreType.DMA
    some = lambda n: pltpu.SemaphoreType.DMA((n,))
    return pl.pallas_call(
        kernel,
        out_shape=[jax.ShapeDtypeStruct(block, F32)] * 2,
        in_specs=[hbm] * 5,
        out_specs=[vmem, vmem],
        scratch_shapes=[
            pltpu.VMEM(block, BF),
            pltpu.VMEM((X, nk) + block, BF),
            pltpu.VMEM((no, nq) + block, BF),
            pltpu.VMEM((X - 1, nk) + block, BF),
            pltpu.VMEM((no, nq - 1) + block, BF),
            pltpu.VMEM((nk,) + block, F32),
            pltpu.VMEM((no,) + block, F32),
            pltpu.VMEM((nk, X - 1) + block, BF),
            pltpu.VMEM((no, nq - 1) + block, BF),
            pltpu.VMEM((nk,) + block, BF),
            pltpu.VMEM((no,) + block, BF),
            pltpu.VMEM((nk,) + block, BF),
            pltpu.VMEM((no,) + block, BF),
            one, some(nk), one, some(no),
            one, one, one, some(no),
            one, some(nk), one, some(no),
            one, some(nk), one, some(no),
            pltpu.VMEM(block, F32),
            pltpu.VMEM(block, F32),
            pltpu.VMEM((labels.shape[0] // 128, 128), jnp.int32),
            pltpu.SMEM((1,), F32),
            pltpu.SMEM((1,), F32),
            some(5),
            pltpu.VMEM((X * nk * rows, width), F32),
            pltpu.SemaphoreType.REGULAR((2,)),
        ],
        compiler_params=pltpu.CompilerParams(
            collective_id=0, has_side_effects=True, vmem_limit_bytes=60 * 2**20
        ),
    )(labels.reshape(-1, 128), scale_logarithm, bias, image_emb, text_emb)


def solution(mesh):
    rows = P(("outer", "inner"), None)
    return jax.shard_map(
        per_device,
        mesh=mesh,
        in_specs=(rows, rows, P(), P(), P()),
        out_specs=(rows, rows),
        check_vma=False,
    )
```

time: 65.6 us -> 63.5 us (0.968)
  the two profiles are of different devices: /device:TPU:2 before, /device:TPU:6 now
where the time goes in v3:
time: 63.5 us; the launch traced here: 62.6 us
  Pallas kernels  58.6 us (92%)
  local copies, waits for them, and re-layouts  2.01 us (3%)
  between operations  1.94 us (3%)
    pallas_call x1, Pallas kernels, per_device(): pl.pallas_call(kernel, out_shape=[jax.ShapeDtypeStruct(block, F32)] * 2,...  58.6 us
    unnamed x4, local copies, waits for them, and re-layouts  2.01 us

profile of v3, /device:TPU:6, one launch (start us, length us, event | category | flops | bytes accessed | tf_op | source)
XLA Modules:
  0.0 62.6 jit_solution(10252902610854054162)
XLA Ops:
  1.9 58.6 %shard_map.68 = (f32[8,1152]{1,0:T(8,128)}, f32[8,1152]{1,0:T(8,128)}) custom-call(s32[64,128]{1,0:T(8,128)} %bitcast.1, f32[1]{0:T(128)S(6)} %copy.9.scale_hbm, f32[1]{0:T(128)S(6)} %copy.10.bias_hbm, f32[8,1152]{1,0:T(8,128)} %image_hbm.1, f32[8,1152]{1,0:T(8,128)} %text_hbm.1), custom_call_target="tpu_custom_call" | custom-call | tf_op jit(solution)/shard_map/pallas_call | solution.py:298
  60.6 0.0 copy-start
  60.6 1.4 %copy.11 = f32[8,1152]{1,0:T(8,128)} copy(f32[8,1152]{1,0:T(8,128)} %get-tuple-element.4) | data formatting | bytes 73728
  62.0 0.0 copy-done
  62.0 0.6 copy.12
Async XLA Ops:
  60.6 1.4 %copy-start = (f32[8,1152]{1,0:T(8,128)S(1)}, f32[8,1152]{1,0:T(8,128)}, u32[]{:S(2)}) copy-start(f32[8,1152]{1,0:T(8,128)} %get-tuple-element.5) | copy-start | bytes 110596

commit v4 on v3

--- a/solution.py
+++ b/solution.py
@@ -99,7 +99,12 @@
     for k, step in sorted(enumerate(TEXT_STEPS), key=lambda w: abs(w[1])):
         if step:
             send(tbuf.at[0, home], tbuf.at[0, k], zt_s, zt_r.at[k], device(dz=side * step))
-    spread_text(home)
+        else:
+            spread_text(home)
+
+    urgent_low = jnp.logical_and(z >= STRIDE, z < 3 * STRIDE)
+    urgent_high = jnp.logical_or(z < STRIDE, z >= Z - STRIDE)
+    urgent_far = jnp.logical_and(z >= 3 * STRIDE, z < Z - STRIDE)
 
     lane = lax.broadcasted_iota(jnp.int32, (rows, 128), 1)
     row = lax.broadcasted_iota(jnp.int32, (rows, 128), 0)
@@ -164,19 +169,21 @@
         wait(tbuf.at[0, k], zt_r.at[k])
         spread_text(k)
 
-    for k, step in enumerate(TEXT_STEPS):
+    for k, step in sorted(enumerate(TEXT_STEPS), key=lambda w: abs(w[1])):
         if 0 < abs(step) <= STRIDE // 2:
             pull_text(k)
-    for o, step in ((1, STRIDE), (2, -STRIDE)):
+    start = jnp.where(urgent_high, 2, 1)
+    for o in (start, 3 - start):
+        step = STRIDE * (3 - 2 * o)
         wait(ibuf.at[o, 0], zi_r.at[o])
         pl.semaphore_wait(ready.at[o - 1], 1)
-        far = 0 if o == 1 else 3
+        far = 3 * (o - 1)
         send(ibuf.at[o, 0], ibuf.at[far, 0], zi_s, zi_r.at[far], device(dz=2 * step))
+    for k, step in sorted(enumerate(TEXT_STEPS), key=lambda w: abs(w[1])):
+        if abs(step) > STRIDE // 2:
+            pull_text(k)
     for o in (1, 2):
         spread_image(o)
-    for k, step in enumerate(TEXT_STEPS):
-        if STRIDE // 2 < abs(step):
-            pull_text(k)
 
     def pull_far():
         for o in far_turns:
@@ -197,10 +204,6 @@
     tnear[...] = lax.dot_general(
         weights, images, (((0,), (0,)), ((), ())), preferred_element_type=F32
     )
-    urgent_low = jnp.logical_and(z >= STRIDE, z < 3 * STRIDE)
-    urgent_high = jnp.logical_or(z < STRIDE, z >= Z - STRIDE)
-    urgent_far = jnp.logical_and(z >= 3 * STRIDE, z < Z - STRIDE)
-
     for n, o in enumerate(far_turns):
         wait(ibuf.at[o, 1:], pi_r.at[o])
         images = as_rows(ibuf[o])
@@ -328,7 +331,7 @@
             pltpu.SemaphoreType.REGULAR((2,)),
         ],
         compiler_params=pltpu.CompilerParams(
-            collective_id=0, has_side_effects=True, vmem_limit_bytes=60 * 2**20
+            collective_id=0, has_side_effects=True, vmem_limit_bytes=55112 * 1024
         ),
     )(labels.reshape(-1, 128), scale_logarithm, bias, image_emb, text_emb)
 

time: 63.5 us -> 62.1 us (0.978)
  Pallas kernels: 58.6 us -> 56.9 us
    pallas_call x1, Pallas kernels: 58.6 us -> 56.9 us  [per_device(): pl.pallas_call(kernel, out_shape=[jax.ShapeDtypeStruct(block, F32)] * 2,...]
where the time goes in v4:
time: 62.1 us; the launch traced here: 60.9 us
  Pallas kernels  56.9 us (92%)
  local copies, waits for them, and re-layouts  1.99 us (3%)
  between operations  1.94 us (3%)
    pallas_call x1, Pallas kernels, per_device(): pl.pallas_call(kernel, out_shape=[jax.ShapeDtypeStruct(block, F32)] * 2,...  56.9 us
    unnamed x4, local copies, waits for them, and re-layouts  1.99 us

profile of v4, /device:TPU:6, one launch (start us, length us, event | category | flops | bytes accessed | tf_op | source)
XLA Modules:
  0.0 60.9 jit_solution(16484284013978603133)
XLA Ops:
  1.9 0.0 copy-start
  1.9 0.7 %copy-done = s32[8192]{0:T(1024)S(1)} copy-done((s32[8192]{0:T(1024)S(1)}, s32[8192]{0:T(1024)}, u32[]{:S(2)}) %copy-start) | copy-done | bytes 32792
  2.7 56.9 %shard_map.68 = (f32[8,1152]{1,0:T(8,128)S(1)}, f32[8,1152]{1,0:T(8,128)S(1)}) custom-call(s32[64,128]{1,0:T(8,128)S(1)} %bitcast.1, f32[1]{0:T(128)S(6)} %copy.9.scale_hbm, f32[1]{0:T(128)S(6)} %copy.10.bias_hbm, f32[8,1152]{1,0:T(8,128)} %image_hbm.1, f32[8,1152]{1,0:T(8,128)} %text_hbm.1), custom_call_target="tpu_custom_call" | custom-call | tf_op jit(solution)/shard_map/pallas_call | solution.py:301
  59.6 0.6 %copy.11 = f32[8,1152]{1,0:T(8,128)} copy(f32[8,1152]{1,0:T(8,128)S(1)} %get-tuple-element.4) | data formatting | bytes 73728
  60.3 0.6 %copy.12 = f32[8,1152]{1,0:T(8,128)} copy(f32[8,1152]{1,0:T(8,128)S(1)} %get-tuple-element.5) | data formatting | bytes 73728
Async XLA Ops:
  1.9 0.8 %copy-start = (s32[8192]{0:T(1024)S(1)}, s32[8192]{0:T(1024)}, u32[]{:S(2)}) copy-start(s32[8192]{0:T(1024)} %param.7) | copy-start | bytes 98308

commit v5 on v4

--- a/solution.py
+++ b/solution.py
@@ -199,8 +199,6 @@
     images = as_rows(ibuf[1:3])
     weights = weigh(images, texts, near_label)
     keep_images(jnp.dot(weights, texts, preferred_element_type=F32), (1, 2))
-    return_image(1)
-    return_image(2)
     tnear[...] = lax.dot_general(
         weights, images, (((0,), (0,)), ((), ())), preferred_element_type=F32
     )
@@ -210,6 +208,9 @@
         weights = weigh(images, texts, far_labels[n])
         keep_images(jnp.dot(weights, texts, preferred_element_type=F32), (o,))
         return_image(o)
+        if n == 1:
+            return_image(start)
+            return_image(3 - start)
         tnear[...] += lax.dot_general(
             weights, images, (((0,), (0,)), ((), ())), preferred_element_type=F32
         )

time: 62.1 us -> 60.3 us (0.971)
  the two profiles are of different devices: /device:TPU:6 before, /device:TPU:9 now
where the time goes in v5:
time: 60.3 us; the launch traced here: 60 us
  Pallas kernels  56 us (93%)
  local copies, waits for them, and re-layouts  1.99 us (3%)
  between operations  1.94 us (3%)
    pallas_call x1, Pallas kernels, per_device(): pl.pallas_call(kernel, out_shape=[jax.ShapeDtypeStruct(block, F32)] * 2,...  56 us
    unnamed x4, local copies, waits for them, and re-layouts  1.99 us

profile of v5, /device:TPU:9, one launch (start us, length us, event | category | flops | bytes accessed | tf_op | source)
XLA Modules:
  0.0 60.0 jit_solution(3516914144109959)
XLA Ops:
  1.9 0.0 copy-start
  1.9 0.7 %copy-done = s32[8192]{0:T(1024)S(1)} copy-done((s32[8192]{0:T(1024)S(1)}, s32[8192]{0:T(1024)}, u32[]{:S(2)}) %copy-start) | copy-done | bytes 32792
  2.7 56.0 %shard_map.68 = (f32[8,1152]{1,0:T(8,128)S(1)}, f32[8,1152]{1,0:T(8,128)S(1)}) custom-call(s32[64,128]{1,0:T(8,128)S(1)} %bitcast.1, f32[1]{0:T(128)S(6)} %copy.9.scale_hbm, f32[1]{0:T(128)S(6)} %copy.10.bias_hbm, f32[8,1152]{1,0:T(8,128)} %image_hbm.1, f32[8,1152]{1,0:T(8,128)} %text_hbm.1), custom_call_target="tpu_custom_call" | custom-call | tf_op jit(solution)/shard_map/pallas_call | solution.py:302
  58.7 0.6 %copy.11 = f32[8,1152]{1,0:T(8,128)} copy(f32[8,1152]{1,0:T(8,128)S(1)} %get-tuple-element.4) | data formatting | bytes 73728
  59.3 0.6 %copy.12 = f32[8,1152]{1,0:T(8,128)} copy(f32[8,1152]{1,0:T(8,128)S(1)} %get-tuple-element.5) | data formatting | bytes 73728
Async XLA Ops:
  1.9 0.8 %copy-start = (s32[8192]{0:T(1024)S(1)}, s32[8192]{0:T(1024)}, u32[]{:S(2)}) copy-start(s32[8192]{0:T(1024)} %param.7) | copy-start | bytes 98308

commit v6 on v4

--- a/solution.py
+++ b/solution.py
@@ -199,8 +199,6 @@
     images = as_rows(ibuf[1:3])
     weights = weigh(images, texts, near_label)
     keep_images(jnp.dot(weights, texts, preferred_element_type=F32), (1, 2))
-    return_image(1)
-    return_image(2)
     tnear[...] = lax.dot_general(
         weights, images, (((0,), (0,)), ((), ())), preferred_element_type=F32
     )
@@ -225,6 +223,9 @@
     for k in text_turns:
         for j in range(1, X):
             send(tsend.at[j - 1, k], tback.at[k, j - 1], rt_s, rt_r.at[k], device(dx=-j))
+
+    return_image(start)
+    return_image(3 - start)
 
     def join_text(k):
         wait(tback.at[k], rt_r.at[k])

time: 62.1 us -> 60.3 us (0.971)
  Pallas kernels: 56.9 us -> 55.2 us
    pallas_call x1, Pallas kernels: 56.9 us -> 55.2 us  [per_device(): pl.pallas_call(kernel, out_shape=[jax.ShapeDtypeStruct(block, F32)] * 2,...]
where the time goes in v6:
time: 60.3 us; the launch traced here: 59.1 us
  Pallas kernels  55.2 us (92%)
  local copies, waits for them, and re-layouts  1.99 us (3%)
  between operations  1.94 us (3%)
    pallas_call x1, Pallas kernels, per_device(): pl.pallas_call(kernel, out_shape=[jax.ShapeDtypeStruct(block, F32)] * 2,...  55.2 us
    unnamed x4, local copies, waits for them, and re-layouts  1.99 us

profile of v6, /device:TPU:6, one launch (start us, length us, event | category | flops | bytes accessed | tf_op | source)
XLA Modules:
  0.0 59.1 jit_solution(16980543568867505095)
XLA Ops:
  1.9 0.0 copy-start
  1.9 0.7 %copy-done = s32[8192]{0:T(1024)S(1)} copy-done((s32[8192]{0:T(1024)S(1)}, s32[8192]{0:T(1024)}, u32[]{:S(2)}) %copy-start) | copy-done | bytes 32792
  2.7 55.2 %shard_map.68 = (f32[8,1152]{1,0:T(8,128)S(1)}, f32[8,1152]{1,0:T(8,128)S(1)}) custom-call(s32[64,128]{1,0:T(8,128)S(1)} %bitcast.1, f32[1]{0:T(128)S(6)} %copy.9.scale_hbm, f32[1]{0:T(128)S(6)} %copy.10.bias_hbm, f32[8,1152]{1,0:T(8,128)} %image_hbm.1, f32[8,1152]{1,0:T(8,128)} %text_hbm.1), custom_call_target="tpu_custom_call" | custom-call | tf_op jit(solution)/shard_map/pallas_call | solution.py:302
  57.9 0.6 %copy.11 = f32[8,1152]{1,0:T(8,128)} copy(f32[8,1152]{1,0:T(8,128)S(1)} %get-tuple-element.4) | data formatting | bytes 73728
  58.5 0.6 %copy.12 = f32[8,1152]{1,0:T(8,128)} copy(f32[8,1152]{1,0:T(8,128)S(1)} %get-tuple-element.5) | data formatting | bytes 73728
Async XLA Ops:
  1.9 0.8 %copy-start = (s32[8192]{0:T(1024)S(1)}, s32[8192]{0:T(1024)}, u32[]{:S(2)}) copy-start(s32[8192]{0:T(1024)} %param.7) | copy-start | bytes 98308
